TPU v7x, 128 devices: a whole 4x4x4 slice. The times are simulated.
128 devices in a mesh: batch: 4 (over z), proto: 32 (over x, y, core).
Axes of the slice: x: 4, y: 4, z: 4, core: 2. Of those that a mesh axis runs over, the one named last changes fastest.
Arguments:
- features: float32 [8192, 256], P(('batch', 'proto')), may hold values from -100 to 100, as said below
- prototypes: bfloat16 [256, 65536], P(None, ('proto', 'batch')), may hold values from -2 to 2, as said below
Outputs:
- targets: float32 [8192, 65536], P('batch', 'proto')
Inputs may be any that keep to these rules, and one draw needn't show every extreme that they name: `features`: real values, bounded by 100 in magnitude. `prototypes`: real values.
All inputs are finite; a program needn't handle non-finite values.
Results may differ from a plain program's by a relative error of at most 0.0026.
Values may be sent and summed in bfloat16 or wider, within the bound.
A program may use at most 64 MiB of HBM per device.

v0:
```python
import functools

import jax
import jax.numpy as jnp
from jax import lax
from jax.experimental import pallas as pl
from jax.experimental.pallas import tpu as pltpu
from jax.sharding import PartitionSpec as P

ITERS = 3
PROTOS = 65536
ROWS = 8192
eps = 1e-06
sharpening_divisor = 0.07
LOG2E = 1.4426950408889634
EXP2_SCALE = LOG2E / sharpening_divisor

NZ = 4
NP = 32
N_ROWS = ROWS // NZ
N_COLS = PROTOS // NP
WIDTH = 256
QCOLS = N_COLS // NZ
FROWS = N_ROWS // NP
BLOCK = 256
HALVES = 2
HALF = N_ROWS // HALVES
TILES = HALF // 128
PCHUNK = WIDTH // 4
SLAB = N_ROWS // 4

MESH = pl.DeviceIdType.MESH


def hops(d):
    return sum(min(v, 4 - v) for v in d[:2])


CHIPS = sorted(((dx, dy) for dx in range(4) for dy in range(4) if dx or dy), key=hops, reverse=True)
PEERS = sorted(
    ((dx, dy, dc) for dx in range(4) for dy in range(4) for dc in range(2) if dx or dy or dc),
    key=hops, reverse=True,
)
NEAR = [(2, 0, 0), (0, 2, 0), (1, 0, 0), (3, 0, 0), (0, 1, 0), (0, 3, 0), (0, 0, 1)]


def operand(dense):
    high = dense.astype(jnp.bfloat16).astype(jnp.float32)
    low = dense - high
    tiles = [
        jnp.concatenate(
            [jnp.broadcast_to(high[i:i + 1], (8, 128)), jnp.broadcast_to(low[i:i + 1], (8, 128))], axis=0
        ).astype(jnp.bfloat16)
        for i in range(dense.shape[0])
    ]
    return jnp.concatenate(tiles, axis=1)


def matvec(parts, matrix):
    return jnp.dot(parts, matrix, preferred_element_type=jnp.float32)


def dense_rows(wide):
    row = lax.broadcasted_iota(jnp.int32, (8, 128), 0)
    out = wide[:, 0:128]
    for i in range(1, wide.shape[1] // 128):
        out = jnp.where(row == i, wide[:, i * 128:(i + 1) * 128], out)
    return out


def join(product):
    return dense_rows(product[0:8] + product[8:16])


def balance_kernel(
    feat_hbm, proto_hbm, f_out, p_out, r_out, c_out,
    feat, proto, fb, ft, pb, pt, e, et, el, col, zs, zr, ps, pr, qs, qr,
    s_in, s_right, s_left, s_fwd, r_left, r_right, r_far,
    s_feat, r_feat, s_sib, r_sib, s_z, r_z, s_p, r_p, s_q, r_q, s_out, greeted,
):
    z = lax.axis_index("batch")
    p = lax.axis_index("proto")
    x, y, core = p // 8, (p // 2) % 4, p % 2
    at_x = [((x + d) % 4) * 8 for d in range(4)]
    at_y = [((y + d) % 4) * 2 for d in range(4)]
    at_core = [core, 1 - core]
    at_z = [(z + d) % 4 for d in range(4)]
    right, far, left = at_z[1], at_z[2], at_z[3]

    def plane(dx, dy, dc):
        return at_x[dx % 4] + at_y[dy % 4] + at_core[dc]

    barrier = pltpu.get_barrier_semaphore()
    for dz in (2, 1, 3):
        pl.semaphore_signal(barrier, inc=1, device_id=(at_z[dz], p), device_id_type=MESH)
    for d in NEAR:
        pl.semaphore_signal(barrier, inc=1, device_id=(z, plane(*d)), device_id_type=MESH)

    proto_in = pltpu.make_async_copy(proto_hbm, proto, s_in.at[0])
    feat_in = pltpu.make_async_copy(feat_hbm, feat, s_in.at[1])
    proto_in.start()
    feat_in.start()

    def rows_of(owner):
        return pl.ds(pl.multiple_of(owner * FROWS, FROWS), FROWS)

    proto_in.wait()
    raw = proto[...].astype(jnp.float32)
    pb[z] = (raw * lax.rsqrt(jnp.sum(raw * raw, axis=0, keepdims=True) + eps)).astype(jnp.bfloat16)
    feat_in.wait()
    raw = feat[...]
    fb[rows_of(p), :] = (
        raw * lax.rsqrt(jnp.sum(raw * raw, axis=1, keepdims=True) + eps)
    ).astype(jnp.bfloat16)

    pl.semaphore_wait(barrier, NZ - 1 + len(NEAR))

    def send(src, dst, send_sem, recv_sem, target):
        pltpu.make_async_remote_copy(
            src_ref=src, dst_ref=dst, send_sem=send_sem, recv_sem=recv_sem,
            device_id=target, device_id_type=MESH,
        ).start()

    def arrived(ref, sem):
        pltpu.make_async_remote_copy(
            src_ref=ref, dst_ref=ref, send_sem=sem, recv_sem=sem,
            device_id=(right, p), device_id_type=MESH,
        ).wait_recv()

    def sent(ref, sem):
        pltpu.make_async_remote_copy(
            src_ref=ref, dst_ref=ref, send_sem=sem, recv_sem=sem,
            device_id=(right, p), device_id_type=MESH,
        ).wait_send()

    def chunk(owner, k):
        return pb.at[owner, pl.ds(k * PCHUNK, PCHUNK), :]

    for k in range(4):
        kr, kl = k, (k + 2) % 4
        send(chunk(z, kr), chunk(z, kr), s_right.at[kr], r_left.at[kr], (right, p))
        send(chunk(z, kl), chunk(z, kl), s_left.at[kl], r_right.at[kl], (left, p))

    sibling = plane(0, 0, 1)
    mine = fb.at[rows_of(p), :]
    def send_features(slabs):
        for n, (dx, dy) in enumerate(CHIPS):
            if dx in slabs:
                send(mine, mine, s_feat.at[n], r_feat.at[n], (z, plane(dx, dy, 0)))

    for dx in (2, 1, 3):
        pl.semaphore_signal(greeted, inc=1, device_id=(z, plane(dx, 0, 0)), device_id_type=MESH)
    send_features((0,))
    send(mine, mine, s_sib.at[15], r_sib.at[15], (z, sibling))
    pl.semaphore_wait(greeted, 3)
    send_features((1, 2, 3))

    def pass_features(slab):
        for n, (dx, dy) in enumerate(CHIPS):
            if dx == slab:
                block = fb.at[rows_of(plane(4 - dx, 4 - dy, 0)), :]
                arrived(block, r_feat.at[n])
                send(block, block, s_sib.at[n], r_sib.at[n], (z, sibling))

    def pass_proto(k):
        arrived(chunk(left, k), r_left.at[k])
        send(chunk(left, k), chunk(left, k), s_fwd.at[k], r_far.at[k], (right, p))
        arrived(chunk(right, k + 2), r_right.at[k + 2])
        send(chunk(right, k + 2), chunk(right, k + 2), s_fwd.at[k + 2], r_far.at[k + 2], (left, p))

    def wait_slab(slab):
        for n, (dx, dy) in enumerate(CHIPS):
            if dx == slab:
                arrived(fb.at[rows_of(plane(4 - dx, 4 - dy, 1)), :], r_sib.at[n])
        if slab == 0:
            arrived(fb.at[rows_of(sibling), :], r_sib.at[15])

    def send_columns(it, q):
        for dz in (2, 1, 3):
            send(zs.at[it, q], zr.at[it, q, dz], s_z.at[it, q], r_z.at[it, q], (at_z[dz], p))

    def score_rows(q, start, count):
        rows = pl.ds(pl.multiple_of(start, count), count)
        s = jnp.dot(fb[rows, :], pb[q], preferred_element_type=jnp.float32)
        t = jnp.exp2(s * EXP2_SCALE)
        e[q, rows, :] = t.astype(jnp.bfloat16)
        return jnp.sum(t.reshape(count // 8, 8, QCOLS), axis=0)

    def score_slab(q, slab):
        return score_rows(q, at_x[(4 - slab) % 4] * (SLAB // 8), SLAB)

    def finish_block(q, total):
        total = jnp.sum(total, axis=0, keepdims=True)
        zs[0, q] = dense_rows(jnp.broadcast_to(total, (8, QCOLS)))
        send_columns(0, q)

    def turn_features():
        ft[...] = fb[...].T

    def score_turned(q, low):
        if not low:
            pt[q] = pb[q].T

        s = jnp.dot(pt[q], ft[...], preferred_element_type=jnp.float32)
        t = jnp.exp2(s * EXP2_SCALE)
        high = t.astype(jnp.bfloat16)
        if low:
            el[q] = (t - high.astype(jnp.float32)).astype(jnp.bfloat16)
        else:
            et[q] = high

    pass_features(0)
    pass_proto(0)
    pass_features(1)
    pass_proto(1)
    pass_features(3)
    wait_slab(0)
    col[0] = score_slab(z, 0)
    wait_slab(1)
    col[0] += score_slab(z, 1)
    pass_features(2)
    wait_slab(3)
    col[0] += score_slab(z, 3)
    for k in (2, 3):
        arrived(chunk(left, k), r_left.at[k])
    for k in (0, 1):
        arrived(chunk(right, k), r_right.at[k])
    for i, q in ((1, left), (2, right)):
        col[i] = score_slab(q, 0) + score_slab(q, 1) + score_slab(q, 3)
    wait_slab(2)
    for i, q in enumerate((z, left, right)):
        finish_block(q, col[i] + score_slab(q, 2))
    for k in range(4):
        arrived(chunk(far, k), r_far.at[k])
    finish_block(far, score_rows(far, 0, N_ROWS))

    f_copy = pltpu.make_async_copy(fb, f_out, s_out.at[0])
    p_copy = pltpu.make_async_copy(pb, p_out, s_out.at[1])
    f_copy.start()
    p_copy.start()
    turn_features()
    for q in (z, left, right, far):
        score_turned(q, False)

    for it in range(ITERS):
        last = it == ITERS - 1
        if it > 0:
            arrived(qr.at[it - 1], r_q.at[it - 1])
            row_sum = qs[it - 1].astype(jnp.float32) + jnp.sum(qr[it - 1].astype(jnp.float32), axis=0)
            parts = operand(1.0 / (ROWS * row_sum))
            for q in range(NZ):
                zs[it, q] = join(matvec(parts, e[q]))
                send_columns(it, q)
        totals = [jnp.zeros((16, HALF), jnp.float32)] * HALVES
        for q in range(NZ):
            arrived(zr.at[it, q, pl.ds(1, NZ - 1)], r_z.at[it, q])
            col_scale = 1.0 / (PROTOS * (zs[it, q] + jnp.sum(zr[it, q, 1:NZ], axis=0)))
            if last:
                c_out[q] = col_scale
            parts = operand(col_scale[0:QCOLS // 128])
            for h in range(HALVES):
                rows = slice(h * HALF, (h + 1) * HALF)
                totals[h] = totals[h] + matvec(parts, et[q, :, rows])
                if last:
                    totals[h] = totals[h] + matvec(parts, el[q, :, rows])
                if last and q == NZ - 1:
                    ps[h] = join(totals[h])
                    for j, d in enumerate(PEERS):
                        send(ps.at[h], pr.at[h, j], s_p.at[h], r_p.at[h], (z, plane(*d)))
        if not last:
            qs[it] = jnp.concatenate([join(t) for t in totals], axis=0).astype(jnp.bfloat16)
            for j, d in enumerate(PEERS):
                send(qs.at[it], qr.at[it, j], s_q.at[it], r_q.at[it], (z, plane(*d)))
        if it == 0:
            for q in range(NZ):
                score_turned(q, True)

    for h in range(HALVES):
        arrived(pr.at[h], r_p.at[h])
        r_out[h] = 1.0 / (ROWS * (ps[h] + jnp.sum(pr[h], axis=0)))

    for k in range(4):
        sent(chunk(z, k), s_right.at[k])
        sent(chunk(z, k), s_left.at[k])
        sent(chunk(z, k), s_fwd.at[k])
    for n in range(15):
        sent(mine, s_feat.at[n])
        sent(mine, s_sib.at[n])
    sent(mine, s_sib.at[15])
    for it in range(ITERS):
        for q in range(NZ):
            sent(zr.at[it, q, pl.ds(1, NZ - 1)], s_z.at[it, q])
    for it in range(ITERS - 1):
        sent(qr.at[it], s_q.at[it])
    for h in range(HALVES):
        sent(pr.at[h], s_p.at[h])
    f_copy.wait()
    p_copy.wait()


def balance(features, prototypes):
    f32, bf16 = jnp.float32, jnp.bfloat16
    vmem = pl.BlockSpec(memory_space=pltpu.VMEM)
    anywhere = pl.BlockSpec(memory_space=pl.ANY)
    hbm = pl.BlockSpec(memory_space=pltpu.HBM)
    dma = pltpu.SemaphoreType.DMA
    return pl.pallas_call(
        balance_kernel,
        out_shape=(
            jax.ShapeDtypeStruct((N_ROWS, WIDTH), bf16),
            jax.ShapeDtypeStruct((NZ, WIDTH, QCOLS), bf16),
            jax.ShapeDtypeStruct((HALVES, 8, 128), f32),
            jax.ShapeDtypeStruct((NZ, 8, 128), f32),
        ),
        in_specs=[hbm, hbm],
        out_specs=(anywhere, anywhere, vmem, vmem),
        scratch_shapes=[
            pltpu.VMEM((FROWS, WIDTH), f32),
            pltpu.VMEM((WIDTH, QCOLS), bf16),
            pltpu.VMEM((N_ROWS, WIDTH), bf16),
            pltpu.VMEM((WIDTH, N_ROWS), bf16),
            pltpu.VMEM((NZ, WIDTH, QCOLS), bf16),
            pltpu.VMEM((NZ, QCOLS, WIDTH), bf16),
            pltpu.VMEM((NZ, N_ROWS, QCOLS), bf16),
            pltpu.VMEM((NZ, QCOLS, N_ROWS), bf16),
            pltpu.VMEM((NZ, QCOLS, N_ROWS), bf16),
            pltpu.VMEM((3, 8, QCOLS), f32),
            pltpu.VMEM((ITERS, NZ, 8, 128), f32),
            pltpu.VMEM((ITERS, NZ, NZ, 8, 128), f32),
            pltpu.VMEM((HALVES, 8, 128), f32),
            pltpu.VMEM((HALVES, NP - 1, 8, 128), f32),
            pltpu.VMEM((ITERS - 1, 16, 128), bf16),
            pltpu.VMEM((ITERS - 1, NP - 1, 16, 128), bf16),
            dma((2,)), dma((4,)), dma((4,)), dma((4,)), dma((4,)), dma((4,)), dma((4,)),
            dma((15,)), dma((15,)), dma((16,)), dma((16,)),
            dma((ITERS, NZ)), dma((ITERS, NZ)), dma((HALVES,)), dma((HALVES,)), dma((ITERS - 1,)), dma((ITERS - 1,)),
            dma((2,)), pltpu.SemaphoreType.REGULAR,
        ],
        compiler_params=pltpu.CompilerParams(
            collective_id=0, has_side_effects=True, vmem_limit_bytes=44 * 2**20
        ),
        cost_estimate=pl.CostEstimate(
            flops=6 * N_ROWS * N_COLS * WIDTH, bytes_accessed=4 * 2**20, transcendentals=3 * N_ROWS * N_COLS
        ),
        name="balance",
    )(*(pltpu.with_memory_space_constraint(a, pltpu.HBM) for a in (features, prototypes)))


def write_kernel(f, p, r, c, out, buf, rc, sem):
    steps = N_ROWS // BLOCK
    turned = [jnp.broadcast_to(r[h, i:i + 1, :], (8, 128)).T[:, 0:1] for h in range(HALVES) for i in range(TILES)]
    rc[...] = jnp.concatenate(turned, axis=0)
    scale = [
        jnp.concatenate([c[q, i:i + 1, :] * float(ROWS * PROTOS) for i in range(QCOLS // 128)], axis=1)
        for q in range(NZ)
    ]

    def store(i):
        return pltpu.make_async_copy(
            buf.at[i], out.at[pl.ds(pl.multiple_of(i * BLOCK, BLOCK), BLOCK), :], sem.at[i]
        )

    def visit(i, carry):
        rows = pl.ds(pl.multiple_of(i * BLOCK, BLOCK), BLOCK)
        for q in range(NZ):
            s = jnp.dot(f[rows, :], p[q], preferred_element_type=jnp.float32)
            buf[i, :, q * QCOLS:(q + 1) * QCOLS] = jnp.exp2(s * EXP2_SCALE) * rc[rows, :] * scale[q]
        store(i).start()
        return carry

    lax.fori_loop(0, steps, visit, 0)
    for i in range(steps):
        store(i).wait()


def write(f, p, r, c):
    vmem = pl.BlockSpec(memory_space=pltpu.VMEM)
    return pl.pallas_call(
        write_kernel,
        out_shape=jax.ShapeDtypeStruct((N_ROWS, N_COLS), jnp.float32),
        in_specs=[vmem] * 4,
        out_specs=pl.BlockSpec(memory_space=pl.ANY),
        scratch_shapes=[
            pltpu.VMEM((N_ROWS // BLOCK, BLOCK, N_COLS), jnp.float32),
            pltpu.VMEM((N_ROWS, 1), jnp.float32),
            pltpu.SemaphoreType.DMA((N_ROWS // BLOCK,)),
        ],
        compiler_params=pltpu.CompilerParams(vmem_limit_bytes=40 * 2**20),
        cost_estimate=pl.CostEstimate(
            flops=2 * N_ROWS * N_COLS * WIDTH, bytes_accessed=18 * 2**20, transcendentals=N_ROWS * N_COLS
        ),
        name="write",
    )(f, p, r, c)


def body(features, prototypes):
    return write(*balance(features, prototypes))


def solution(mesh):
    in_specs = (P(("batch", "proto"), None), P(None, ("proto", "batch")))
    out_specs = P("batch", "proto")
    return jax.shard_map(body, mesh=mesh, in_specs=in_specs, out_specs=out_specs, check_vma=False)
```

profile of v0, /device:TPU:1, one launch (start us, length us, event | category | flops | bytes accessed | tf_op | source)
XLA Modules:
  0.0 59.8 jit_solution(8988991075175779122)
XLA Ops:
  0.0 52.8 %balance.1 = (bf16[2048,256]{1,0:T(8,128)(2,1)S(1)}, bf16[4,256,512]{2,1,0:T(8,128)(2,1)S(1)}, f32[2,8,128]{2,1,0:T(8,128)S(1)}, f32[4,8,128]{2,1,0:T(8,128)S(1)}) custom-call(f32[64,256]{1,0:T(8,128)} %feat_hbm.1, bf16[256,512]{1,0:T(8,128)(2,1)} %proto_hbm.1), custom_call_target="tpu_custom_call" | custom-call | flops 6442450944 | bytes 4194304 | tf_op jit(solution)/shard_map/balance/pallas_call | solution.py:307
  52.8 6.8 %write.1 = f32[2048,2048]{1,0:T(8,128)} custom-call(bf16[2048,256]{1,0:T(8,128)(2,1)S(1)} %get-tuple-element.9.f, bf16[4,256,512]{2,1,0:T(8,128)(2,1)S(1)} %get-tuple-element.10.p, f32[2,8,128]{2,1,0:T(8,128)S(1)} %get-tuple-element.11.r, f32[4,8,128]{2,1,0:T(8,128)S(1)} %get-tuple-element.12.c), custom_call_target="tpu_custom_call" | custom-call | flops 2147483648 | bytes 18874368 | tf_op jit(solution)/shard_map/write/pallas_call | solution.py:378
where the time goes:
time: 59.9 us; the launch traced here: 59.8 us
  Pallas kernels  59.6 us (99%)
    pallas_call x1, Pallas kernels, balance(): pl.pallas_call(balance_kernel, out_shape=(jax.ShapeDtypeStruct((N_ROWS, W...  52.8 us
    pallas_call x1, Pallas kernels, write(): pl.pallas_call(write_kernel, out_shape=jax.ShapeDtypeStruct((N_ROWS, N_CO...  6.75 us

commit v1 on v0

--- a/solution.py
+++ b/solution.py
@@ -264,9 +264,10 @@
                 if last:
                     totals[h] = totals[h] + matvec(parts, el[q, :, rows])
                 if last and q == NZ - 1:
-                    ps[h] = join(totals[h])
-                    for j, d in enumerate(PEERS):
-                        send(ps.at[h], pr.at[h, j], s_p.at[h], r_p.at[h], (z, plane(*d)))
+                    ps[h * 8:(h + 1) * 8, :] = join(totals[h])
+        if last:
+            for j, d in enumerate(PEERS):
+                send(ps, pr.at[j], s_p, r_p, (z, plane(*d)))
         if not last:
             qs[it] = jnp.concatenate([join(t) for t in totals], axis=0).astype(jnp.bfloat16)
             for j, d in enumerate(PEERS):
@@ -274,10 +275,6 @@
         if it == 0:
             for q in range(NZ):
                 score_turned(q, True)
-
-    for h in range(HALVES):
-        arrived(pr.at[h], r_p.at[h])
-        r_out[h] = 1.0 / (ROWS * (ps[h] + jnp.sum(pr[h], axis=0)))
 
     for k in range(4):
         sent(chunk(z, k), s_right.at[k])
@@ -292,10 +289,15 @@
             sent(zr.at[it, q, pl.ds(1, NZ - 1)], s_z.at[it, q])
     for it in range(ITERS - 1):
         sent(qr.at[it], s_q.at[it])
-    for h in range(HALVES):
-        sent(pr.at[h], s_p.at[h])
     f_copy.wait()
     p_copy.wait()
+
+    arrived(pr, r_p)
+    scale = 1.0 / (ROWS * (ps[...] + jnp.sum(pr[...], axis=0)))
+    for h in range(HALVES):
+        r_out[h] = scale[h * 8:(h + 1) * 8]
+
+    sent(pr, s_p)
 
 
 def balance(features, prototypes):
@@ -327,13 +329,13 @@
             pltpu.VMEM((3, 8, QCOLS), f32),
             pltpu.VMEM((ITERS, NZ, 8, 128), f32),
             pltpu.VMEM((ITERS, NZ, NZ, 8, 128), f32),
-            pltpu.VMEM((HALVES, 8, 128), f32),
-            pltpu.VMEM((HALVES, NP - 1, 8, 128), f32),
+            pltpu.VMEM((16, 128), f32),
+            pltpu.VMEM((NP - 1, 16, 128), f32),
             pltpu.VMEM((ITERS - 1, 16, 128), bf16),
             pltpu.VMEM((ITERS - 1, NP - 1, 16, 128), bf16),
             dma((2,)), dma((4,)), dma((4,)), dma((4,)), dma((4,)), dma((4,)), dma((4,)),
             dma((15,)), dma((15,)), dma((16,)), dma((16,)),
-            dma((ITERS, NZ)), dma((ITERS, NZ)), dma((HALVES,)), dma((HALVES,)), dma((ITERS - 1,)), dma((ITERS - 1,)),
+            dma((ITERS, NZ)), dma((ITERS, NZ)), pltpu.SemaphoreType.DMA, pltpu.SemaphoreType.DMA, dma((ITERS - 1,)), dma((ITERS - 1,)),
             dma((2,)), pltpu.SemaphoreType.REGULAR,
         ],
         compiler_params=pltpu.CompilerParams(

time: 59.9 us -> 59.6 us (level)
  no operation moved by 1% of the time
where the time goes in v1:
time: 59.6 us; the launch traced here: 59.4 us
  Pallas kernels  59.3 us (99%)
    pallas_call x1, Pallas kernels, balance(): pl.pallas_call(balance_kernel, out_shape=(jax.ShapeDtypeStruct((N_ROWS, W...  52.5 us
    pallas_call x1, Pallas kernels, write(): pl.pallas_call(write_kernel, out_shape=jax.ShapeDtypeStruct((N_ROWS, N_CO...  6.75 us

profile of v1, /device:TPU:1, one launch (start us, length us, event | category | flops | bytes accessed | tf_op | source)
XLA Modules:
  0.0 59.4 jit_solution(16398607890144033623)
XLA Ops:
  0.0 52.5 %balance.1 = (bf16[2048,256]{1,0:T(8,128)(2,1)S(1)}, bf16[4,256,512]{2,1,0:T(8,128)(2,1)S(1)}, f32[2,8,128]{2,1,0:T(8,128)S(1)}, f32[4,8,128]{2,1,0:T(8,128)S(1)}) custom-call(f32[64,256]{1,0:T(8,128)} %feat_hbm.1, bf16[256,512]{1,0:T(8,128)(2,1)} %proto_hbm.1), custom_call_target="tpu_custom_call" | custom-call | flops 6442450944 | bytes 4194304 | tf_op jit(solution)/shard_map/balance/pallas_call | solution.py:309
  52.5 6.8 %write.1 = f32[2048,2048]{1,0:T(8,128)} custom-call(bf16[2048,256]{1,0:T(8,128)(2,1)S(1)} %get-tuple-element.9.f, bf16[4,256,512]{2,1,0:T(8,128)(2,1)S(1)} %get-tuple-element.10.p, f32[2,8,128]{2,1,0:T(8,128)S(1)} %get-tuple-element.11.r, f32[4,8,128]{2,1,0:T(8,128)S(1)} %get-tuple-element.12.c), custom_call_target="tpu_custom_call" | custom-call | flops 2147483648 | bytes 18874368 | tf_op jit(solution)/shard_map/write/pallas_call | solution.py:380

commit v2 on v1

--- a/solution.py
+++ b/solution.py
@@ -107,39 +107,43 @@
     proto_in.wait()
     raw = proto[...].astype(jnp.float32)
     pb[z] = (raw * lax.rsqrt(jnp.sum(raw * raw, axis=0, keepdims=True) + eps)).astype(jnp.bfloat16)
+
+    pl.semaphore_wait(barrier, NZ - 1 + len(NEAR))
+
+    def send(src, dst, send_sem, recv_sem, target):
+        pltpu.make_async_remote_copy(
+            src_ref=src, dst_ref=dst, send_sem=send_sem, recv_sem=recv_sem,
+            device_id=target, device_id_type=MESH,
+        ).start()
+
+    def arrived(ref, sem):
+        pltpu.make_async_remote_copy(
+            src_ref=ref, dst_ref=ref, send_sem=sem, recv_sem=sem,
+            device_id=(right, p), device_id_type=MESH,
+        ).wait_recv()
+
+    def sent(ref, sem):
+        pltpu.make_async_remote_copy(
+            src_ref=ref, dst_ref=ref, send_sem=sem, recv_sem=sem,
+            device_id=(right, p), device_id_type=MESH,
+        ).wait_send()
+
+    def chunk(owner, k):
+        return pb.at[owner, pl.ds(k * PCHUNK, PCHUNK), :]
+
+    for dx in (2, 1, 3):
+        pl.semaphore_signal(greeted, inc=1, device_id=(z, plane(dx, 0, 0)), device_id_type=MESH)
+
+    for k in range(4):
+        kr, kl = k, (k + 2) % 4
+        send(chunk(z, kr), chunk(z, kr), s_right.at[kr], r_left.at[kr], (right, p))
+        send(chunk(z, kl), chunk(z, kl), s_left.at[kl], r_right.at[kl], (left, p))
+
     feat_in.wait()
     raw = feat[...]
     fb[rows_of(p), :] = (
         raw * lax.rsqrt(jnp.sum(raw * raw, axis=1, keepdims=True) + eps)
     ).astype(jnp.bfloat16)
-
-    pl.semaphore_wait(barrier, NZ - 1 + len(NEAR))
-
-    def send(src, dst, send_sem, recv_sem, target):
-        pltpu.make_async_remote_copy(
-            src_ref=src, dst_ref=dst, send_sem=send_sem, recv_sem=recv_sem,
-            device_id=target, device_id_type=MESH,
-        ).start()
-
-    def arrived(ref, sem):
-        pltpu.make_async_remote_copy(
-            src_ref=ref, dst_ref=ref, send_sem=sem, recv_sem=sem,
-            device_id=(right, p), device_id_type=MESH,
-        ).wait_recv()
-
-    def sent(ref, sem):
-        pltpu.make_async_remote_copy(
-            src_ref=ref, dst_ref=ref, send_sem=sem, recv_sem=sem,
-            device_id=(right, p), device_id_type=MESH,
-        ).wait_send()
-
-    def chunk(owner, k):
-        return pb.at[owner, pl.ds(k * PCHUNK, PCHUNK), :]
-
-    for k in range(4):
-        kr, kl = k, (k + 2) % 4
-        send(chunk(z, kr), chunk(z, kr), s_right.at[kr], r_left.at[kr], (right, p))
-        send(chunk(z, kl), chunk(z, kl), s_left.at[kl], r_right.at[kl], (left, p))
 
     sibling = plane(0, 0, 1)
     mine = fb.at[rows_of(p), :]
@@ -148,8 +152,6 @@
             if dx in slabs:
                 send(mine, mine, s_feat.at[n], r_feat.at[n], (z, plane(dx, dy, 0)))
 
-    for dx in (2, 1, 3):
-        pl.semaphore_signal(greeted, inc=1, device_id=(z, plane(dx, 0, 0)), device_id_type=MESH)
     send_features((0,))
     send(mine, mine, s_sib.at[15], r_sib.at[15], (z, sibling))
     pl.semaphore_wait(greeted, 3)

time: 59.6 us -> 59.6 us (level)
  no operation moved by 1% of the time
where the time goes in v2:
time: 59.6 us; the launch traced here: 59.4 us
  Pallas kernels  59.3 us (99%)
    pallas_call x1, Pallas kernels, balance(): pl.pallas_call(balance_kernel, out_shape=(jax.ShapeDtypeStruct((N_ROWS, W...  52.5 us
    pallas_call x1, Pallas kernels, write(): pl.pallas_call(write_kernel, out_shape=jax.ShapeDtypeStruct((N_ROWS, N_CO...  6.75 us

profile of v2, /device:TPU:1, one launch (start us, length us, event | category | flops | bytes accessed | tf_op | source)
XLA Modules:
  0.0 59.4 jit_solution(2138691103997105470)
XLA Ops:
  0.0 52.5 %balance.1 = (bf16[2048,256]{1,0:T(8,128)(2,1)S(1)}, bf16[4,256,512]{2,1,0:T(8,128)(2,1)S(1)}, f32[2,8,128]{2,1,0:T(8,128)S(1)}, f32[4,8,128]{2,1,0:T(8,128)S(1)}) custom-call(f32[64,256]{1,0:T(8,128)} %feat_hbm.1, bf16[256,512]{1,0:T(8,128)(2,1)} %proto_hbm.1), custom_call_target="tpu_custom_call" | custom-call | flops 6442450944 | bytes 4194304 | tf_op jit(solution)/shard_map/balance/pallas_call | solution.py:311
  52.5 6.8 %write.1 = f32[2048,2048]{1,0:T(8,128)} custom-call(bf16[2048,256]{1,0:T(8,128)(2,1)S(1)} %get-tuple-element.9.f, bf16[4,256,512]{2,1,0:T(8,128)(2,1)S(1)} %get-tuple-element.10.p, f32[2,8,128]{2,1,0:T(8,128)S(1)} %get-tuple-element.11.r, f32[4,8,128]{2,1,0:T(8,128)S(1)} %get-tuple-element.12.c), custom_call_target="tpu_custom_call" | custom-call | flops 2147483648 | bytes 18874368 | tf_op jit(solution)/shard_map/write/pallas_call | solution.py:382
